TPU v7x, 32 devices: a whole 2x2x4 slice. The times are simulated.
32 devices in a mesh: groups: 2 (over y), expert: 4 (over z), tensor: 2 (over x), pair: 2 (over core).
Axes of the slice: x: 2, y: 2, z: 4, core: 2. Of those that a mesh axis runs over, the one named last changes fastest.
Arguments:
- hidden: bfloat16 [384, 3584], P(('groups', 'expert'), ('tensor', 'pair')), parts along dimension 0, may hold values from -6 to 6
- routes: int32 [384, 8], P(('groups', 'expert')), parts along dimension 0, may hold values from 0 to 31, all different within a row; in each aligned block of 48 rows (0 to 47, 48 to 95, ...) at most 18 rows name the same one
- w_router: bfloat16 [3584, 32], P(('tensor', 'pair')), may hold values from -0.09375 to 0.09375
- w_gate: bfloat16 [32, 3584, 1024], P('expert', None, ('tensor', 'pair')), may hold values from -0.09375 to 0.09375
- w_up: bfloat16 [32, 3584, 1024], P('expert', None, ('tensor', 'pair')), may hold values from -0.09375 to 0.09375
- w_down: bfloat16 [32, 1024, 3584], P('expert', ('tensor', 'pair')), may hold values from -0.1875 to 0.1875
Outputs:
- layer_out: bfloat16 [384, 3584], P(('groups', 'expert'), ('tensor', 'pair')), parts along dimension 0
There are 2 independent parts, one for each index of `groups`. A program takes and returns all parts, laid end to end along the dimension named above; an argument that names none is the same for every part. Nothing has to cross between parts.
Inputs may be any that keep to these rules, and one draw needn't show every extreme that they name: `routes`: each row names 8 different experts. Among the 48 rows of one device (aligned blocks) no expert is named by more than 18 rows, a bound that some block reaches.
All inputs are finite; a program needn't handle non-finite values.
Results may differ from a plain program's by a relative error of at most 0.0075.
Values may be sent and summed in bfloat16 or wider, within the bound.
A program may use at most 192 MiB of HBM per device.

v0:
```python
import jax
import jax.numpy as jnp
from jax import lax
from jax.sharding import PartitionSpec as P

CAP = 18


route_scale = 2.5


def experts_apply(received, w_gate, w_up, w_down):
    gate_act = jnp.einsum("ecsd,edf->ecsf", received, w_gate, preferred_element_type=jnp.float32)
    up_act = jnp.einsum("ecsd,edf->ecsf", received, w_up, preferred_element_type=jnp.float32)
    hidden_act = (jax.nn.silu(gate_act) * up_act).astype(jnp.bfloat16)
    down_act = jnp.einsum("ecsf,efd->ecsd", hidden_act, w_down, preferred_element_type=jnp.float32)
    return down_act.astype(jnp.bfloat16)


def per_device(hidden, routes, w_router, w_gate, w_up, w_down):
    row_count = hidden.shape[0]
    top_count = routes.shape[1]
    experts = w_router.shape[1]
    slot_total = experts * CAP
    flat_routes = routes.reshape(-1)
    expert_ids = lax.iota(jnp.int32, experts)
    onehot = (flat_routes[:, None] == expert_ids[None, :]).astype(jnp.int32)
    running = jnp.cumsum(onehot, axis=0) - 1
    slot_index = jnp.sum(running * onehot, axis=1)
    target = flat_routes * CAP + slot_index
    placed = (target[:, None] == lax.iota(jnp.int32, slot_total)[None, :]).reshape(
        row_count, top_count, slot_total
    )
    dispatch_matrix = jnp.any(placed, axis=1).astype(jnp.bfloat16)
    full_rows, router_full = (
        lax.all_gather(hidden, ("tensor", "pair"), axis=1, tiled=True),
        lax.all_gather(w_router, ("tensor", "pair"), axis=0, tiled=True),
    )
    logits = jnp.dot(full_rows, router_full, preferred_element_type=jnp.float32)
    outbound = jnp.einsum(
        "rs,rd->sd", dispatch_matrix, full_rows, preferred_element_type=jnp.float32
    )
    outbound = outbound.astype(jnp.bfloat16).reshape(experts, 1, CAP, full_rows.shape[1])
    partial_value = experts_apply(
        lax.all_to_all(outbound, "expert", split_axis=0, concat_axis=1, tiled=True),
        w_gate,
        w_up,
        w_down,
    )
    scores = jax.nn.sigmoid(logits)
    route_hits = (routes[:, :, None] == expert_ids[None, None, :]).astype(jnp.float32)
    chosen = jnp.sum(scores[:, None, :] * route_hits, axis=2)
    gate_values = (route_scale * chosen / jnp.sum(chosen, axis=1, keepdims=True)).astype(
        jnp.bfloat16
    )
    summed = (
        lax.psum_scatter(partial_value, ("tensor", "pair"), scatter_dimension=3, tiled=True)
        .astype(jnp.float32)
        .astype(jnp.bfloat16)
    )
    returned = lax.all_to_all(summed, "expert", split_axis=1, concat_axis=0, tiled=True)
    expert_rows = returned.reshape(slot_total, returned.shape[3])
    combine_matrix = jnp.sum(placed.astype(jnp.bfloat16) * gate_values[:, :, None], axis=1)
    combined = jnp.dot(combine_matrix, expert_rows, preferred_element_type=jnp.float32)
    return (hidden.astype(jnp.float32) + combined).astype(jnp.bfloat16)


def solution(mesh):
    in_specs = (
        P(("groups", "expert"), ("tensor", "pair")),
        P(("groups", "expert"), None),
        P(("tensor", "pair"), None),
        P("expert", None, ("tensor", "pair")),
        P("expert", None, ("tensor", "pair")),
        P("expert", ("tensor", "pair"), None),
    )
    out_specs = P(("groups", "expert"), ("tensor", "pair"))
    return jax.shard_map(
        per_device, mesh=mesh, in_specs=in_specs, out_specs=out_specs, check_vma=False
    )
```

profile of v0, /device:TPU:0, one launch (start us, length us, event | category | flops | bytes accessed | tf_op | source)
XLA Modules:
  0.0 384.8 jit_solution(16192527618572920830)
XLA Ops:
  6.5 0.8 copy.43
  7.5 0.9 reduce-window.6
  8.4 0.2 slice_reduce_fusion
  8.9 0.7 multiply_add_fusion
  9.7 0.4 fusion.27
  10.1 7.9 %all_gather.6 = bf16[48,3584]{1,0:T(8,128)(2,1)S(1)} all-gather(bf16[48,896]{1,0:T(8,128)(2,1)} %param.6), channel_id=1, replica_groups=mesh['groups'=2,'expert'=4,'tensor'=2,'pair'=2] {'tensor','pair'}, dimensions={1}, use_global_device_ids=true | all-gather | bytes 430080 | tf_op jit(solution)/shard_map/all_gather | solution.py:36
  17.9 3.3 convolution_convert_fusion
  21.2 7.2 %reshape.67 = bf16[32,1,18,3584]{3,2,0,1:T(8,128)(2,1)} reshape(bf16[576,3584]{1,0:T(8,128)(2,1)} %convolution_convert_fusion) | data formatting | bytes 8257536 | tf_op jit(solution)/shard_map/reshape | solution.py:43
  28.4 126.6 %all_to_all.33 = bf16[32,1,18,3584]{3,2,1,0:T(8,128)(2,1)S(1)} all-to-all(bf16[32,1,18,3584]{3,2,1,0:T(8,128)(2,1)} %bitcast.68), channel_id=1, replica_groups=mesh['groups'=2,'expert'=4,'tensor'=2,'pair'=2] {'expert'}, dimensions={0} | all-to-all | bytes 8257536 | tf_op jit(solution)/shard_map/all_to_all | solution.py:45
  155.0 7.8 %fusion.4 = f32[8,4,18,256]{3,2,1,0:T(8,128)S(1)} fusion(bf16[8,3584,256]{2,1,0:T(8,128)(2,1)} %param.9, bf16[4,8,1,18,3584]{4,3,1,0,2:T(8,128)(2,1)S(1)} %bitcast.66), kind=kOutput, calls=%fused_computation.4 | convolution fusion | flops 1056964608 | bytes 19398656 | tf_op jit(solution)/shard_map/ecsd,edf->ecsf/dot_general | solution.py:13
  162.8 7.9 %fusion.18 = bf16[8,4,18,256]{3,2,1,0:T(8,128)(2,1)S(1)} fusion(bf16[8,3584,256]{2,1,0:T(8,128)(2,1)} %param.10, bf16[4,8,1,18,3584]{4,3,1,0,2:T(8,128)(2,1)S(1)} %bitcast.67, f32[8,4,18,256]{3,2,1,0:T(8,128)S(1)} %fusion.4), kind=kOutput, calls=%fused_computation.13 | convolution fusion | flops 1057849344 | bytes 19693568 | tf_op jit(solution)/shard_map/ecsd,edf->ecsf/dot_general | solution.py:14
  170.8 10.1 %fusion.6 = bf16[8,4,18,3584]{3,2,1,0:T(8,128)(2,1)} fusion(bf16[8,4,18,256]{3,2,1,0:T(8,128)(2,1)S(1)} %fusion.18, bf16[8,256,3584]{2,1,0:T(8,128)(2,1)} %param.11), kind=kOutput, calls=%fused_computation.6 | convolution fusion | flops 1059028992 | bytes 19103744 | tf_op jit(solution)/shard_map/ecsf,efd->ecsd/dot_general | solution.py:16
  180.9 36.7 %copy.59 = bf16[8,4,18,3584]{2,1,0,3:T(4,128)(2,1)} copy(bf16[8,4,18,3584]{3,2,1,0:T(8,128)(2,1)} %fusion.6) | data formatting | bytes 8257536
  217.5 52.4 %reshape.72 = bf16[3584,576]{1,0:T(8,128)(2,1)} reshape(bf16[3584,8,4,18]{3,2,1,0:T(4,128)(2,1)} %bitcast.64) | data formatting | bytes 8257536
  269.9 46.1 %reduce-scatter.4.cloned.1.call-done = bf16[896,576]{1,0:T(8,128)(2,1)} async-done(((bf16[3584,576]{1,0:T(8,128)(2,1)}), bf16[896,576]{1,0:T(8,128)(2,1)}) %reduce-scatter.4.cloned.1.call-update) | async-done | bytes 1032208
  316.0 19.6 %reshape.73 = bf16[896,8,4,18]{3,2,1,0:T(4,128)(2,1)} reshape(bf16[896,576]{1,0:T(8,128)(2,1)} %reduce-scatter.4.cloned.1.call-done) | data formatting | bytes 2064384
  335.6 10.8 %copy.52 = bf16[8,4,18,896]{3,0,2,1:T(8,128)(2,1)} copy(bf16[8,4,18,896]{2,1,0,3:T(4,128)(2,1)} %bitcast.65) | data formatting | bytes 2064384 | tf_op jit(solution)/shard_map/reduce_scatter | solution.py:57
  346.4 4.7 %all-to-all-start.1 = ((bf16[8,4,18,896]{3,0,2,1:T(8,128)(2,1)}), bf16[8,4,18,896]{3,0,2,1:T(8,128)(2,1)S(1)}, u32[]{:S(2)}, u32[]{:S(2)}) async-start(bf16[8,4,18,896]{3,0,2,1:T(8,128)(2,1)} %copy.52), calls=%async_computation.1 | async-start | bytes 2064384 | tf_op jit(solution)/shard_map/all_to_all | solution.py:61
  351.1 5.7 %all_gather.7 = bf16[3584,32]{0,1:T(8,128)(2,1)S(1)} all-gather(bf16[896,32]{0,1:T(8,128)(2,1)S(1)} %copy-done.1), channel_id=1, replica_groups=mesh['groups'=2,'expert'=4,'tensor'=2,'pair'=2] {'tensor','pair'}, dimensions={0}, use_global_device_ids=true | all-gather | bytes 286720 | tf_op jit(solution)/shard_map/all_gather | solution.py:37
  356.8 0.2 fusion.26
  357.2 0.4 fusion.29
  357.6 18.9 %all-to-all-done.1 = bf16[8,4,18,896]{3,0,2,1:T(8,128)(2,1)S(1)} async-done(((bf16[8,4,18,896]{3,0,2,1:T(8,128)(2,1)}), bf16[8,4,18,896]{3,0,2,1:T(8,128)(2,1)S(1)}, u32[]{:S(2)}, u32[]{:S(2)}) %all-to-all-start.1) | async-done | bytes 1032224 | tf_op jit(solution)/shard_map/all_to_all | solution.py:61
  376.7 0.4 reshape.68
  377.0 0.9 fusion.23
  (20 shorter events, 0.9 us)
Async XLA Ops:
  6.5 309.5 %reduce-scatter.4.cloned.1.call-start = ((), (), s32[]{:S(2)}) async-start(), calls=%async_computation.3 | async-start | bytes 5734400
  335.6 15.5 %copy-start.1 = (bf16[896,32]{0,1:T(8,128)(2,1)S(1)}, bf16[896,32]{0,1:T(8,128)(2,1)}, u32[]{:S(2)}) copy-start(bf16[896,32]{0,1:T(8,128)(2,1)} %param.8) | copy-start | bytes 172036
  335.6 21.4 %copy-start.2 = (s32[48,8]{0,1:T(8,128)S(1)}, s32[48,8]{0,1:T(8,128)}, u32[]{:S(2)}) copy-start(s32[48,8]{0,1:T(8,128)} %param.7) | copy-start | bytes 4612
  346.4 30.6 %copy-start = (bf16[48,896]{1,0:T(8,128)(2,1)S(1)}, bf16[48,896]{1,0:T(8,128)(2,1)}, u32[]{:S(2)}) copy-start(bf16[48,896]{1,0:T(8,128)(2,1)} %param.6) | copy-start | bytes 258052
  346.4 30.1 %all-to-all-start.1 = ((bf16[8,4,18,896]{3,0,2,1:T(8,128)(2,1)}), bf16[8,4,18,896]{3,0,2,1:T(8,128)(2,1)S(1)}, u32[]{:S(2)}, u32[]{:S(2)}) async-start(bf16[8,4,18,896]{3,0,2,1:T(8,128)(2,1)} %copy.52), calls=%async_computation.1 | async-start | bytes 2064384 | tf_op jit(solution)/shard_map/all_to_all | solution.py:61
Sparse Core Ops, SparseCore 0:
  270.1 45.9 reduce-scatter.3
where the time goes:
time: 387 us; the launch traced here: 385 us
  blocking collectives  140 us (36%)
  local copies, waits for them, and re-layouts  129 us (33%)
  waiting for transfers between devices  65 us (17%)
  matrix products  30.3 us (8%)
  between operations  13.5 us (3%)
  starting transfers between devices  4.74 us (1%)
    all_to_all x1, blocking collectives, per_device(): lax.all_to_all(outbound, 'expert', split_axis=0, concat_axis=1, tiled=True)  127 us
    unnamed x10, local copies, waits for them, and re-layouts  109 us
    unnamed x2, waiting for transfers between devices  46.1 us
    all_to_all x1, waiting for transfers between devices, per_device(): lax.all_to_all(summed, 'expert', split_axis=1, concat_axis=0, tiled=True)  18.9 us
    reduce_scatter x1, local copies, waits for them, and re-layouts, per_device(): lax.psum_scatter(partial_value, ('tensor', 'pair'), scatter_dimension=3,...  10.8 us
    dot_general x1, matrix products, experts_apply(): jnp.einsum('ecsf,efd->ecsd', hidden_act, w_down, preferred_element_type=j...  10.1 us
    dot_general x1, matrix products, experts_apply(): jnp.einsum('ecsd,edf->ecsf', received, w_up, preferred_element_type=jnp.f...  7.93 us
    all_gather x1, blocking collectives, per_device(): lax.all_gather(hidden, ('tensor', 'pair'), axis=1, tiled=True)  7.85 us
  transfers between devices with their start and end apart: 2, of which 2 were waited for; matrix products, arithmetic and copies ran while one was open for 0% of the time, Pallas kernels for 0%

commit v1 on v0

--- a/solution.py
+++ b/solution.py
@@ -1,6 +1,10 @@
+import functools
+
 import jax
 import jax.numpy as jnp
 from jax import lax
+from jax.experimental import pallas as pl
+from jax.experimental.pallas import tpu as pltpu
 from jax.sharding import PartitionSpec as P
 
 CAP = 18
@@ -17,7 +21,7 @@
     return down_act.astype(jnp.bfloat16)
 
 
-def per_device(hidden, routes, w_router, w_gate, w_up, w_down):
+def per_device_general(hidden, routes, w_router, w_gate, w_up, w_down):
     row_count = hidden.shape[0]
     top_count = routes.shape[1]
     experts = w_router.shape[1]
@@ -65,6 +69,268 @@
     return (hidden.astype(jnp.float32) + combined).astype(jnp.bfloat16)
 
 
+MESH = pl.DeviceIdType.MESH
+
+
+def fused_kernel(
+    n_expert,
+    hidden_ref, routes_ref, router_ref, gate_hbm, up_hbm, down_hbm, out_ref,
+    wg, wu, wd, xbuf, acc, act, logit_buf, gate_buf,
+    ybuf, pair_in, xsum, x_in, zsum, z_in,
+    w_sem, l_send, l_recv, g_send, g_recv,
+    zx_send, zx_recv, px_send, px_recv, xx_send, xx_recv, dx_send, dx_recv,
+    py_send, py_recv, xy_send, xy_recv, zy_send, zy_recv,
+):
+    rows, width = hidden_ref.shape
+    local, depth, units = wg.shape
+    half = depth // 2
+    experts = router_ref.shape[1]
+    grp, z = lax.axis_index("groups"), lax.axis_index("expert")
+    t, p = lax.axis_index("tensor"), lax.axis_index("pair")
+    z_at = [lax.rem(z + d, n_expert) for d in range(n_expert)]
+    col = t * 2 + p
+
+    def dev(zz, tt, pp):
+        return (grp, zz, tt, pp)
+
+    pair_dev, x_dev, diag_dev = dev(z, t, 1 - p), dev(z, 1 - t, p), dev(z, 1 - t, 1 - p)
+
+    def row_ds(zz):
+        return pl.ds(pl.multiple_of(zz * rows, 16), rows)
+
+    def col_ds(tt, pp):
+        return pl.ds(pl.multiple_of((tt * 2 + pp) * width, 128), width)
+
+    def half_rows(h):
+        tt = t if h == 0 else 1 - t
+        return pl.ds(pl.multiple_of(tt * half, 128), half)
+
+    def load_in(h, m, e):
+        source, target = ((gate_hbm, wg), (up_hbm, wu))[m]
+        where = half_rows(h)
+        return pltpu.make_async_copy(source.at[e, where, :], target.at[e, where, :], w_sem.at[h * 2 + m, e])
+
+    def load_down(e):
+        return pltpu.make_async_copy(down_hbm.at[e], wd.at[e], w_sem.at[4, e])
+
+    @pl.loop(0, local)
+    def _(e):
+        load_in(0, 0, e).start()
+        load_in(0, 1, e).start()
+
+    @pl.loop(0, local)
+    def _(e):
+        load_in(1, 0, e).start()
+        load_in(1, 1, e).start()
+
+    @pl.loop(0, local)
+    def _(e):
+        load_down(e).start()
+
+    barrier = pltpu.get_barrier_semaphore()
+    peers = [pair_dev, x_dev, diag_dev] + [dev(zz, t, p) for zz in z_at[1:]]
+    for peer in peers:
+        pl.semaphore_signal(barrier, inc=1, device_id=peer, device_id_type=MESH)
+    pl.semaphore_wait(barrier, len(peers))
+
+    sends = []
+
+    def send(source, target, send_sem, recv_sem, device):
+        copy = pltpu.make_async_remote_copy(
+            src_ref=source, dst_ref=target, send_sem=send_sem, recv_sem=recv_sem,
+            device_id=device, device_id_type=MESH,
+        )
+        copy.start()
+        sends.append(copy)
+
+    def arrived(target, send_sem, recv_sem, device):
+        pltpu.make_async_remote_copy(
+            src_ref=target, dst_ref=target, send_sem=send_sem, recv_sem=recv_sem,
+            device_id=device, device_id_type=MESH,
+        ).wait_recv()
+
+    for d in range(n_expert - 1, 0, -1):
+        send(hidden_ref, xbuf.at[row_ds(z), col_ds(t, p)], zx_send.at[d], zx_recv.at[z], dev(z_at[d], t, p))
+    send(hidden_ref, xbuf.at[row_ds(z), col_ds(t, p)], xx_send.at[0], xx_recv.at[z], x_dev)
+    send(hidden_ref, xbuf.at[row_ds(z), col_ds(t, p)], px_send.at[0], px_recv.at[z], pair_dev)
+    xbuf[row_ds(z), col_ds(t, p)] = hidden_ref[...]
+
+    logit_buf[col] = jnp.dot(hidden_ref[...], router_ref[...], preferred_element_type=jnp.float32)
+    for i, peer in enumerate((pair_dev, x_dev, diag_dev)):
+        send(logit_buf.at[col], logit_buf.at[col], l_send.at[i], l_recv.at[col], peer)
+
+    for d in range(1, n_expert):
+        zz = z_at[d]
+        block = xbuf.at[row_ds(zz), col_ds(t, p)]
+        arrived(block, zx_send.at[d], zx_recv.at[zz], dev(zz, t, p))
+        send(block, block, xx_send.at[d], xx_recv.at[zz], x_dev)
+        send(block, block, px_send.at[d], px_recv.at[zz], pair_dev)
+
+    for i, (tt, pp) in enumerate(((t, 1 - p), (1 - t, p), (1 - t, 1 - p))):
+        c = tt * 2 + pp
+        arrived(logit_buf.at[c], l_send.at[i], l_recv.at[c], dev(z, tt, pp))
+    logits = (logit_buf[0] + logit_buf[1]) + (logit_buf[2] + logit_buf[3])
+    scores = 1.0 / (1.0 + jnp.exp(-logits))
+    ids = lax.broadcasted_iota(jnp.int32, (rows, experts), 1)
+    picks = routes_ref[...]
+    chosen = jnp.zeros((rows, experts), jnp.float32)
+    for k in range(picks.shape[1]):
+        chosen = chosen + jnp.where(picks[:, k:k + 1] == ids, scores, 0.0)
+    gates = route_scale * chosen / jnp.sum(chosen, axis=1, keepdims=True)
+    gate_buf[z] = gates.astype(jnp.bfloat16).astype(jnp.float32)
+    for d in range(1, n_expert):
+        send(gate_buf.at[z], gate_buf.at[z], g_send.at[d], g_recv.at[z], dev(z_at[d], t, p))
+
+    for d in range(n_expert):
+        zz = z_at[d]
+        arrived(xbuf.at[row_ds(zz), col_ds(t, 1 - p)], px_send.at[d], px_recv.at[zz], pair_dev)
+    near = pl.ds(pl.multiple_of(t * half, 128), half)
+    far = pl.ds(pl.multiple_of((1 - t) * half, 128), half)
+
+    def first(e, carry):
+        load_in(0, 0, e).wait()
+        acc[0, e] = jnp.dot(xbuf[:, near], wg[e, half_rows(0), :], preferred_element_type=jnp.float32)
+        load_in(0, 1, e).wait()
+        acc[1, e] = jnp.dot(xbuf[:, near], wu[e, half_rows(0), :], preferred_element_type=jnp.float32)
+        return carry
+
+    step = local // n_expert
+    for d in range(n_expert):
+        lax.fori_loop(d * step, (d + 1) * step if d < n_expert - 1 else local, first, 0)
+        zz = z_at[d]
+        block = xbuf.at[row_ds(zz), col_ds(1 - t, p)]
+        arrived(block, xx_send.at[d], xx_recv.at[zz], x_dev)
+        send(block, block, dx_send.at[d], dx_recv.at[zz], pair_dev)
+    for d in range(n_expert):
+        zz = z_at[d]
+        arrived(xbuf.at[row_ds(zz), col_ds(1 - t, 1 - p)], dx_send.at[d], dx_recv.at[zz], pair_dev)
+    for d in range(1, n_expert):
+        zz = z_at[d]
+        arrived(gate_buf.at[zz], g_send.at[d], g_recv.at[zz], dev(zz, t, p))
+
+    all_rows = n_expert * rows
+    lanes = lax.broadcasted_iota(jnp.int32, (all_rows, experts), 1)
+
+    def second(e, carry):
+        load_in(1, 0, e).wait()
+        gate_act = acc[0, e] + jnp.dot(xbuf[:, far], wg[e, half_rows(1), :], preferred_element_type=jnp.float32)
+        load_in(1, 1, e).wait()
+        up_act = acc[1, e] + jnp.dot(xbuf[:, far], wu[e, half_rows(1), :], preferred_element_type=jnp.float32)
+        table = gate_buf[...].reshape(all_rows, experts)
+        weight = jnp.sum(jnp.where(lanes == z * local + e, table, 0.0), axis=1, keepdims=True)
+        value = gate_act / (1.0 + jnp.exp(-gate_act)) * up_act * weight
+        act[:, pl.ds(pl.multiple_of(e * units, 128), units)] = value.astype(jnp.bfloat16)
+        return carry
+
+    lax.fori_loop(0, local, second, 0)
+
+    @pl.loop(0, local)
+    def _(e):
+        load_down(e).wait()
+
+    tile = 256 if half % 256 == 0 else 128
+    for h in range(2):
+        tt = 1 - t if h == 0 else t
+
+        def down(n, carry):
+            source = pl.ds(pl.multiple_of(tt * half + n * tile, 128), tile)
+            weights = wd[:, :, source].reshape(local * units, tile)
+            value = jnp.dot(act[...], weights, preferred_element_type=jnp.float32)
+            ybuf[h, :, pl.ds(pl.multiple_of(n * tile, 128), tile)] = value.astype(jnp.bfloat16)
+            return carry
+
+        lax.fori_loop(0, half // tile, down, 0)
+        other = pl.ds(pl.multiple_of((1 - p) * width, 128), width)
+        send(ybuf.at[h, :, other], pair_in.at[h], py_send.at[h], py_recv.at[h], pair_dev)
+        if h == 0:
+            continue
+        mine = pl.ds(pl.multiple_of(p * width, 128), width)
+        arrived(pair_in.at[0], py_send.at[0], py_recv.at[0], pair_dev)
+        for d in [*range(1, n_expert), 0]:
+            zz = z_at[d]
+            part = ybuf[0, row_ds(zz), mine].astype(jnp.float32) + pair_in[0, row_ds(zz), :].astype(jnp.float32)
+            xsum[zz] = part.astype(jnp.bfloat16)
+            send(xsum.at[zz], x_in.at[zz], xy_send.at[d], xy_recv.at[zz], x_dev)
+        arrived(pair_in.at[1], py_send.at[1], py_recv.at[1], pair_dev)
+
+    def own_sum(zz, d):
+        arrived(x_in.at[zz], xy_send.at[d], xy_recv.at[zz], x_dev)
+        part = ybuf[1, row_ds(zz), mine].astype(jnp.float32) + pair_in[1, row_ds(zz), :].astype(jnp.float32)
+        return part + x_in[zz].astype(jnp.float32)
+
+    for d in range(1, n_expert):
+        zz = z_at[d]
+        zsum[zz] = own_sum(zz, d).astype(jnp.bfloat16)
+        send(zsum.at[zz], z_in.at[z], zy_send.at[d], zy_recv.at[z], dev(zz, t, p))
+    total = hidden_ref[...].astype(jnp.float32) + own_sum(z, 0)
+    for d in range(n_expert - 1, 0, -1):
+        zz = z_at[d]
+        arrived(z_in.at[zz], zy_send.at[d], zy_recv.at[zz], dev(zz, t, p))
+        total = total + z_in[zz].astype(jnp.float32)
+    out_ref[...] = total.astype(jnp.bfloat16)
+    for copy in sends:
+        copy.wait_send()
+
+
+def fused(n_expert, hidden, routes, w_router, w_gate, w_up, w_down):
+    rows, width = hidden.shape
+    local, depth, units = w_gate.shape
+    experts = w_router.shape[1]
+    all_rows = n_expert * rows
+    half = depth // 2
+    vmem = pl.BlockSpec(memory_space=pltpu.VMEM)
+    far = pl.BlockSpec(memory_space=pl.ANY)
+    bf16, f32 = jnp.bfloat16, jnp.float32
+
+    def dma(*shape):
+        return pltpu.SemaphoreType.DMA(shape)
+
+    n = n_expert
+    return pl.pallas_call(
+        functools.partial(fused_kernel, n_expert),
+        out_shape=jax.ShapeDtypeStruct((rows, width), bf16),
+        in_specs=[vmem, vmem, vmem, far, far, far],
+        out_specs=vmem,
+        scratch_shapes=[
+            pltpu.VMEM((local, depth, units), bf16),
+            pltpu.VMEM((local, depth, units), bf16),
+            pltpu.VMEM((local, units, depth), bf16),
+            pltpu.VMEM((all_rows, depth), bf16),
+            pltpu.VMEM((2, local, all_rows, units), f32),
+            pltpu.VMEM((all_rows, local * units), bf16),
+            pltpu.VMEM((4, rows, experts), f32),
+            pltpu.VMEM((n, rows, experts), f32),
+            pltpu.VMEM((2, all_rows, half), bf16),
+            pltpu.VMEM((2, all_rows, width), bf16),
+            pltpu.VMEM((n, rows, width), bf16),
+            pltpu.VMEM((n, rows, width), bf16),
+            pltpu.VMEM((n, rows, width), bf16),
+            pltpu.VMEM((n, rows, width), bf16),
+            dma(5, local), dma(3), dma(4), dma(n), dma(n),
+            dma(n), dma(n), dma(n), dma(n), dma(n), dma(n), dma(n), dma(n),
+            dma(2), dma(2), dma(n), dma(n), dma(n), dma(n),
+        ],
+        compiler_params=pltpu.CompilerParams(
+            collective_id=0, has_side_effects=True, vmem_limit_bytes=58 * 1024 * 1024
+        ),
+        cost_estimate=pl.CostEstimate(
+            flops=6 * all_rows * local * depth * units,
+            bytes_accessed=6 * local * depth * units,
+            transcendentals=all_rows * local * units,
+        ),
+    )(hidden, routes, w_router, w_gate, w_up, w_down)
+
+
+def per_device(n_expert, n_tensor, n_pair, hidden, routes, w_router, w_gate, w_up, w_down):
+    rows, width = hidden.shape
+    local, depth, units = w_gate.shape
+    held = 2 * 3 * local * depth * units
+    fits = held <= 44 * 1024 * 1024 and local % n_expert == 0
+    if n_tensor == 2 and n_pair == 2 and width % 128 == 0 and units % 128 == 0 and rows % 16 == 0 and fits:
+        return fused(n_expert, hidden, routes, w_router, w_gate, w_up, w_down)
+    return per_device_general(hidden, routes, w_router, w_gate, w_up, w_down)
+
+
 def solution(mesh):
     in_specs = (
         P(("groups", "expert"), ("tensor", "pair")),
@@ -76,5 +342,6 @@
     )
     out_specs = P(("groups", "expert"), ("tensor", "pair"))
     return jax.shard_map(
-        per_device, mesh=mesh, in_specs=in_specs, out_specs=out_specs, check_vma=False
-    )
+        functools.partial(per_device, mesh.shape["expert"], mesh.shape["tensor"], mesh.shape["pair"]),
+        mesh=mesh, in_specs=in_specs, out_specs=out_specs, check_vma=False
+    )

time: 387 us -> 56.9 us (0.15)
  blocking collectives: 140 us -> 0 us
  local copies, waits for them, and re-layouts: 129 us -> 4.53 us
  waiting for transfers between devices: 65 us -> 0 us
  Pallas kernels: 0 us -> 52.1 us
  matrix products: 30.3 us -> 0 us
  between operations: 13.5 us -> 0.01 us
  starting transfers between devices: 4.74 us -> 0 us
    all_to_all x1 -> x0, blocking collectives: 127 us -> none  [per_device(): lax.all_to_all(outbound, 'expert', split_axis=0, concat_axis=1, tiled=True)]
    unnamed x10 -> x3, local copies, waits for them, and re-layouts: 109 us -> 4.53 us
    pallas_call x0 -> x1, Pallas kernels: none -> 52.1 us  [fused(): pl.pallas_call(functools.partial(fused_kernel, n_expert), out_shape=jax.S...]
    unnamed x2 -> x0, waiting for transfers between devices: 46.1 us -> none
    dot_general x6 -> x0, matrix products: 30.3 us -> none  [the longest x1 10.1 us: experts_apply(): jnp.einsum('ecsf,efd->ecsd', hidden_act, w_down, preferred_element_type=j...]
    all_to_all x1 -> x0, waiting for transfers between devices: 18.9 us -> none  [per_device(): lax.all_to_all(summed, 'expert', split_axis=1, concat_axis=0, tiled=True)]
    all_gather x2 -> x0, blocking collectives: 13.5 us -> none  [the longest x1 7.85 us: per_device(): lax.all_gather(hidden, ('tensor', 'pair'), axis=1, tiled=True)]
    reduce_scatter x1 -> x0, local copies, waits for them, and re-layouts: 10.8 us -> none  [per_device(): lax.psum_scatter(partial_value, ('tensor', 'pair'), scatter_dimension=3,...]
  transfers between devices with their start and end apart: 2 -> 0, of which waited for: 2 -> 0; matrix products, arithmetic and copies ran while one was open for 0% -> 0% of each run, Pallas kernels for 0% -> 0%
where the time goes in v1:
time: 56.9 us; the launch traced here: 56.7 us
  Pallas kernels  52.1 us (92%)
  local copies, waits for them, and re-layouts  4.53 us (8%)
    pallas_call x1, Pallas kernels, fused(): pl.pallas_call(functools.partial(fused_kernel, n_expert), out_shape=jax.S...  52.1 us
    unnamed x3, local copies, waits for them, and re-layouts  4.53 us

profile of v1, /device:TPU:0, one launch (start us, length us, event | category | flops | bytes accessed | tf_op | source)
XLA Modules:
  0.0 56.7 jit_solution(8073985959013598520)
XLA Ops:
  0.0 1.4 %copy.7.routes_ref = s32[48,8]{1,0:T(8,128)} copy(s32[48,8]{0,1:T(8,128)} %param.7) | data formatting | bytes 3072 | tf_op args[1]
  1.4 1.6 %copy.8.router_ref = bf16[896,32]{1,0:T(8,128)(2,1)} copy(bf16[896,32]{0,1:T(8,128)(2,1)} %param.8) | data formatting | bytes 114688 | tf_op args[2]
  3.0 52.1 %shard_map.64 = bf16[48,896]{1,0:T(8,128)(2,1)} custom-call(bf16[48,896]{1,0:T(8,128)(2,1)} %hidden_ref.1, s32[48,8]{1,0:T(8,128)} %copy.7.routes_ref, bf16[896,32]{1,0:T(8,128)(2,1)} %copy.8.router_ref, bf16[8,3584,256]{2,1,0:T(8,128)(2,1)} %gate_hbm.1, bf16[8,3584,256]{2,1,0:T(8,128)(2,1)} %up_hbm.1, bf16[8,256,3584]{2,1,0:T(8,128)(2,1)} %down_hbm.1), custom_call_target="tpu_custom_call" | custom-call | flops 8455716864 | bytes 44040192 | tf_op jit(solution)/shard_map/pallas_call | solution.py:289
  55.1 1.5 %copy.10 = bf16[48,896]{1,0:T(8,128)(2,1)} copy(bf16[48,896]{1,0:T(8,128)(2,1)} %shard_map.64) | data formatting | bytes 172032

commit v2 on v1

--- a/solution.py
+++ b/solution.py
@@ -84,10 +84,10 @@
     rows, width = hidden_ref.shape
     local, depth, units = wg.shape
     half = depth // 2
-    experts = router_ref.shape[1]
+    experts = router_ref.shape[0]
     grp, z = lax.axis_index("groups"), lax.axis_index("expert")
     t, p = lax.axis_index("tensor"), lax.axis_index("pair")
-    z_at = [lax.rem(z + d, n_expert) for d in range(n_expert)]
+    z_at = [z, z + 1 - 2 * lax.rem(z, 2), lax.rem(z + 2, 4), 3 - z]
     col = t * 2 + p
 
     def dev(zz, tt, pp):
@@ -149,13 +149,15 @@
             device_id=device, device_id_type=MESH,
         ).wait_recv()
 
-    for d in range(n_expert - 1, 0, -1):
-        send(hidden_ref, xbuf.at[row_ds(z), col_ds(t, p)], zx_send.at[d], zx_recv.at[z], dev(z_at[d], t, p))
     send(hidden_ref, xbuf.at[row_ds(z), col_ds(t, p)], xx_send.at[0], xx_recv.at[z], x_dev)
     send(hidden_ref, xbuf.at[row_ds(z), col_ds(t, p)], px_send.at[0], px_recv.at[z], pair_dev)
+    for d in range(1, n_expert):
+        send(hidden_ref, xbuf.at[row_ds(z), col_ds(t, p)], zx_send.at[d], zx_recv.at[z], dev(z_at[d], t, p))
     xbuf[row_ds(z), col_ds(t, p)] = hidden_ref[...]
 
-    logit_buf[col] = jnp.dot(hidden_ref[...], router_ref[...], preferred_element_type=jnp.float32)
+    logit_buf[col] = lax.dot_general(
+        router_ref[...], hidden_ref[...], (((1,), (1,)), ((), ())), preferred_element_type=jnp.float32
+    )
     for i, peer in enumerate((pair_dev, x_dev, diag_dev)):
         send(logit_buf.at[col], logit_buf.at[col], l_send.at[i], l_recv.at[col], peer)
 
@@ -171,13 +173,13 @@
         arrived(logit_buf.at[c], l_send.at[i], l_recv.at[c], dev(z, tt, pp))
     logits = (logit_buf[0] + logit_buf[1]) + (logit_buf[2] + logit_buf[3])
     scores = 1.0 / (1.0 + jnp.exp(-logits))
-    ids = lax.broadcasted_iota(jnp.int32, (rows, experts), 1)
+    ids = lax.broadcasted_iota(jnp.int32, (experts, rows), 0)
     picks = routes_ref[...]
-    chosen = jnp.zeros((rows, experts), jnp.float32)
-    for k in range(picks.shape[1]):
-        chosen = chosen + jnp.where(picks[:, k:k + 1] == ids, scores, 0.0)
-    gates = route_scale * chosen / jnp.sum(chosen, axis=1, keepdims=True)
-    gate_buf[z] = gates.astype(jnp.bfloat16).astype(jnp.float32)
+    chosen = jnp.zeros((experts, rows), jnp.float32)
+    for k in range(picks.shape[0]):
+        chosen = chosen + jnp.where(picks[k:k + 1, :] == ids, scores, 0.0)
+    gates = route_scale * chosen / jnp.sum(chosen, axis=0, keepdims=True)
+    gate_buf[z] = jnp.transpose(gates.astype(jnp.bfloat16).astype(jnp.float32))
     for d in range(1, n_expert):
         send(gate_buf.at[z], gate_buf.at[z], g_send.at[d], g_recv.at[z], dev(z_at[d], t, p))
 
@@ -196,7 +198,7 @@
 
     step = local // n_expert
     for d in range(n_expert):
-        lax.fori_loop(d * step, (d + 1) * step if d < n_expert - 1 else local, first, 0)
+        lax.fori_loop(d * step, (d + 1) * step if d < n_expert - 1 else local, first, 0, unroll=True)
         zz = z_at[d]
         block = xbuf.at[row_ds(zz), col_ds(1 - t, p)]
         arrived(block, xx_send.at[d], xx_recv.at[zz], x_dev)
@@ -222,52 +224,62 @@
         act[:, pl.ds(pl.multiple_of(e * units, 128), units)] = value.astype(jnp.bfloat16)
         return carry
 
-    lax.fori_loop(0, local, second, 0)
+    lax.fori_loop(0, local, second, 0, unroll=True)
 
     @pl.loop(0, local)
     def _(e):
         load_down(e).wait()
 
-    tile = 256 if half % 256 == 0 else 128
+    def down(k, tt, pp, start, size):
+        for begin in range(start, start + size, 256):
+            count = min(256, start + size - begin)
+            source = pl.ds(pl.multiple_of((tt * 2 + pp) * width + begin, 128), count)
+            weights = wd[:, :, source].reshape(local * units, count)
+            value = jnp.dot(act[...], weights, preferred_element_type=jnp.float32)
+            ybuf[k, :, pl.ds(begin, count)] = value.astype(jnp.bfloat16)
+
+    cut = width // 256 * 128 + 128 if width % 256 else width // 2
+    parts = ((0, cut), (cut, width - cut))
+
+    def pair_sum(h, i, zz):
+        where = pl.ds(*parts[i])
+        return ybuf[2 * h + 1, row_ds(zz), where].astype(jnp.float32) + pair_in[h, row_ds(zz), where].astype(jnp.float32)
+
     for h in range(2):
         tt = 1 - t if h == 0 else t
-
-        def down(n, carry):
-            source = pl.ds(pl.multiple_of(tt * half + n * tile, 128), tile)
-            weights = wd[:, :, source].reshape(local * units, tile)
-            value = jnp.dot(act[...], weights, preferred_element_type=jnp.float32)
-            ybuf[h, :, pl.ds(pl.multiple_of(n * tile, 128), tile)] = value.astype(jnp.bfloat16)
-            return carry
-
-        lax.fori_loop(0, half // tile, down, 0)
-        other = pl.ds(pl.multiple_of((1 - p) * width, 128), width)
-        send(ybuf.at[h, :, other], pair_in.at[h], py_send.at[h], py_recv.at[h], pair_dev)
-        if h == 0:
-            continue
-        mine = pl.ds(pl.multiple_of(p * width, 128), width)
-        arrived(pair_in.at[0], py_send.at[0], py_recv.at[0], pair_dev)
-        for d in [*range(1, n_expert), 0]:
+        for i, (start, size) in enumerate(parts):
+            where = pl.ds(start, size)
+            down(2 * h, tt, 1 - p, start, size)
+            landing = pair_in.at[h, :, where]
+            send(ybuf.at[2 * h, :, where], landing, py_send.at[h, i], py_recv.at[h, i], pair_dev)
+            down(2 * h + 1, tt, p, start, size)
+            arrived(landing, py_send.at[h, i], py_recv.at[h, i], pair_dev)
+            if h == 1:
+                continue
+            for d in (1, 2, 3, 0):
+                zz = z_at[d]
+                xsum[zz, :, where] = pair_sum(0, i, zz).astype(jnp.bfloat16)
+                send(xsum.at[zz, :, where], x_in.at[zz, :, where], xy_send.at[i, d], xy_recv.at[i, zz], x_dev)
+
+    def own_sum(zz, d, i):
+        where = pl.ds(*parts[i])
+        arrived(x_in.at[zz, :, where], xy_send.at[i, d], xy_recv.at[i, zz], x_dev)
+        return pair_sum(1, i, zz) + x_in[zz, :, where].astype(jnp.float32)
+
+    for i in range(2):
+        where = pl.ds(*parts[i])
+        for d in range(1, n_expert):
             zz = z_at[d]
-            part = ybuf[0, row_ds(zz), mine].astype(jnp.float32) + pair_in[0, row_ds(zz), :].astype(jnp.float32)
-            xsum[zz] = part.astype(jnp.bfloat16)
-            send(xsum.at[zz], x_in.at[zz], xy_send.at[d], xy_recv.at[zz], x_dev)
-        arrived(pair_in.at[1], py_send.at[1], py_recv.at[1], pair_dev)
-
-    def own_sum(zz, d):
-        arrived(x_in.at[zz], xy_send.at[d], xy_recv.at[zz], x_dev)
-        part = ybuf[1, row_ds(zz), mine].astype(jnp.float32) + pair_in[1, row_ds(zz), :].astype(jnp.float32)
-        return part + x_in[zz].astype(jnp.float32)
-
-    for d in range(1, n_expert):
-        zz = z_at[d]
-        zsum[zz] = own_sum(zz, d).astype(jnp.bfloat16)
-        send(zsum.at[zz], z_in.at[z], zy_send.at[d], zy_recv.at[z], dev(zz, t, p))
-    total = hidden_ref[...].astype(jnp.float32) + own_sum(z, 0)
-    for d in range(n_expert - 1, 0, -1):
-        zz = z_at[d]
-        arrived(z_in.at[zz], zy_send.at[d], zy_recv.at[zz], dev(zz, t, p))
-        total = total + z_in[zz].astype(jnp.float32)
-    out_ref[...] = total.astype(jnp.bfloat16)
+            zsum[zz, :, where] = own_sum(zz, d, i).astype(jnp.bfloat16)
+            send(zsum.at[zz, :, where], z_in.at[z, :, where], zy_send.at[i, d], zy_recv.at[i, z], dev(zz, t, p))
+    for i in range(2):
+        where = pl.ds(*parts[i])
+        total = hidden_ref[:, where].astype(jnp.float32) + own_sum(z, 0, i)
+        for d in range(1, n_expert):
+            zz = z_at[d]
+            arrived(z_in.at[zz, :, where], zy_send.at[i, d], zy_recv.at[i, zz], dev(zz, t, p))
+            total = total + z_in[zz, :, where].astype(jnp.float32)
+        out_ref[:, where] = total.astype(jnp.bfloat16)
     for copy in sends:
         copy.wait_send()
 
@@ -298,9 +310,9 @@
             pltpu.VMEM((all_rows, depth), bf16),
             pltpu.VMEM((2, local, all_rows, units), f32),
             pltpu.VMEM((all_rows, local * units), bf16),
-            pltpu.VMEM((4, rows, experts), f32),
+            pltpu.VMEM((4, experts, rows), f32),
             pltpu.VMEM((n, rows, experts), f32),
-            pltpu.VMEM((2, all_rows, half), bf16),
+            pltpu.VMEM((4, all_rows, width), bf16),
             pltpu.VMEM((2, all_rows, width), bf16),
             pltpu.VMEM((n, rows, width), bf16),
             pltpu.VMEM((n, rows, width), bf16),
@@ -308,7 +320,7 @@
             pltpu.VMEM((n, rows, width), bf16),
             dma(5, local), dma(3), dma(4), dma(n), dma(n),
             dma(n), dma(n), dma(n), dma(n), dma(n), dma(n), dma(n), dma(n),
-            dma(2), dma(2), dma(n), dma(n), dma(n), dma(n),
+            dma(2, 2), dma(2, 2), dma(2, n), dma(2, n), dma(2, n), dma(2, n),
         ],
         compiler_params=pltpu.CompilerParams(
             collective_id=0, has_side_effects=True, vmem_limit_bytes=58 * 1024 * 1024
@@ -318,14 +330,14 @@
             bytes_accessed=6 * local * depth * units,
             transcendentals=all_rows * local * units,
         ),
-    )(hidden, routes, w_router, w_gate, w_up, w_down)
+    )(hidden, routes.T, w_router.T, w_gate, w_up, w_down)
 
 
 def per_device(n_expert, n_tensor, n_pair, hidden, routes, w_router, w_gate, w_up, w_down):
     rows, width = hidden.shape
     local, depth, units = w_gate.shape
     held = 2 * 3 * local * depth * units
-    fits = held <= 44 * 1024 * 1024 and local % n_expert == 0
+    fits = held <= 44 * 1024 * 1024 and n_expert == 4 and local % n_expert == 0
     if n_tensor == 2 and n_pair == 2 and width % 128 == 0 and units % 128 == 0 and rows % 16 == 0 and fits:
         return fused(n_expert, hidden, routes, w_router, w_gate, w_up, w_down)
     return per_device_general(hidden, routes, w_router, w_gate, w_up, w_down)

time: 56.9 us -> 51.5 us (0.905)
  local copies, waits for them, and re-layouts: 4.53 us -> 1.53 us
  Pallas kernels: 52.1 us -> 49.8 us
    unnamed x3 -> x1, local copies, waits for them, and re-layouts: 4.53 us -> 1.53 us
    pallas_call x1, Pallas kernels: 52.1 us -> 49.8 us  [fused(): pl.pallas_call(functools.partial(fused_kernel, n_expert), out_shape=jax.S...]
where the time goes in v2:
time: 51.5 us; the launch traced here: 51.3 us
  Pallas kernels  49.8 us (97%)
  local copies, waits for them, and re-layouts  1.53 us (3%)
    pallas_call x1, Pallas kernels, fused(): pl.pallas_call(functools.partial(fused_kernel, n_expert), out_shape=jax.S...  49.8 us
    unnamed x1, local copies, waits for them, and re-layouts  1.53 us

profile of v2, /device:TPU:0, one launch (start us, length us, event | category | flops | bytes accessed | tf_op | source)
XLA Modules:
  0.0 51.3 jit_solution(7447829541724501035)
XLA Ops:
  0.0 49.8 %shard_map.64 = bf16[48,896]{1,0:T(8,128)(2,1)} custom-call(bf16[48,896]{1,0:T(8,128)(2,1)} %hidden_ref.1, s32[8,48]{1,0:T(8,128)} %bitcast.3, bf16[32,896]{1,0:T(8,128)(2,1)} %bitcast.2, bf16[8,3584,256]{2,1,0:T(8,128)(2,1)} %gate_hbm.1, bf16[8,3584,256]{2,1,0:T(8,128)(2,1)} %up_hbm.1, bf16[8,256,3584]{2,1,0:T(8,128)(2,1)} %down_hbm.1), custom_call_target="tpu_custom_call" | custom-call | flops 8455716864 | bytes 44040192 | tf_op jit(solution)/shard_map/pallas_call | solution.py:301
  49.8 1.5 %copy.8 = bf16[48,896]{1,0:T(8,128)(2,1)} copy(bf16[48,896]{1,0:T(8,128)(2,1)} %shard_map.64) | data formatting | bytes 172032
